TPU v7x, 32 devices: a whole 2x2x4 slice. The times are simulated.
32 devices in a mesh: shot: 8 (over z, y), sub: 4 (over x, core).
Axes of the slice: x: 2, y: 2, z: 4, core: 2. Of those that a mesh axis runs over, the one named last changes fastest.
Arguments:
- background: float32 [3, 64, 192, 128], P(None, 'shot', 'sub'), may hold values from 0.55 to 2.4, as said below
- lanczos: float32 [3, 64, 192, 128], P(None, 'shot', 'sub'), may hold values from -6 to 6
- incident: float32 [8, 9, 16, 192, 128], P('shot', None, 'sub'), may hold values from -6 to 6
- receivers: int32 [8, 4, 256], P('shot', 'sub'), may hold values from 0 to 98303
- anchors: int32 [8], P('shot'), may hold values from 0 to 6, as said below
Outputs:
- hessian_vector: float32 [3, 64, 192, 128], P(None, 'shot', 'sub')
Inputs may be any that keep to these rules, and one draw needn't show every extreme that they name: The footprint of shot s starts at model tile anchors[s], with s - 2 <= anchors[s] <= s; the last shot's footprint starts at tile 8 - 2. Channel 0 of background (first Lame parameter) lies within 1.2 to 2.4, channel 1 (shear modulus) within 0.6 to 1.2, channel 2 (buoyancy) within 0.55 to 1.1.
All inputs are finite; a program needn't handle non-finite values.
Results may differ from a plain program's by a relative error of at most 0.0003.
Values sent between devices are 32-bit elements; how exact they have to be, the bound alone decides.
A program may use at most 128 MiB of HBM per device.

v0:
```python
import functools

import jax
import jax.numpy as jnp
from jax import lax
from jax.experimental import pallas as pl
from jax.experimental.pallas import tpu as pltpu
from jax.sharding import PartitionSpec as P

STEPS = 4
BLOCK = 32
PAD = 8
time_step = 0.25
CHANNELS = (2, 5, 0, 1, 3, 4)
STRESS_FROM = (0, 3, 4, 1, 5, 2)


def kernel(
    shots, subs, back, lan, inc, gap, rec_row, rec_col, out,
    wv, ws, bv, bs, av, st, hist, rec, cnt, prm, img,
    gapp, ub, db, sb, yb, pp, gb, yout, yin, dout, din, uout, uin,
    load_sem, gap_sem, zup_sem, zdn_sem, y_sem, q_sem, loc_sem, rim_sem,
    gq_sem, gloc_sem, gy_sem, gd_sem, gu_sem,
):
    s = lax.axis_index("shot")
    me = lax.axis_index("sub")
    partner = s + 1 - 2 * (s % 2)
    even = s % 2 == 0
    odd = s % 2 == 1
    has_up = s + 2 < shots
    has_dn = s >= 2
    has_above = me + 1 < subs
    has_below = me >= 1
    rows_y = prm.shape[2]
    share = rows_y // subs
    slab = prm.shape[1]
    body = pl.ds(PAD, rows_y)

    def remote(src, dst, sems, index, device):
        return pltpu.make_async_remote_copy(
            src_ref=src, dst_ref=dst, send_sem=sems.at[(0,) + index], recv_sem=sems.at[(1,) + index],
            device_id=device, device_id_type=pl.DeviceIdType.MESH,
        )

    loads = [pltpu.make_async_copy(inc.at[f], wv.at[f, pl.ds(0, slab), body], load_sem.at[f]) for f in range(3)]
    loads += [
        pltpu.make_async_copy(inc.at[3 + STRESS_FROM[f]], ws.at[f, pl.ds(1, slab), body], load_sem.at[3 + f])
        for f in range(6)
    ]
    for load in loads:
        load.start()

    barrier = pltpu.get_barrier_semaphore()
    for k in range(1, subs):
        pl.semaphore_signal(barrier, inc=1, device_id={"sub": lax.rem(me + k, subs)}, device_id_type=pl.DeviceIdType.MESH)
    pl.semaphore_signal(barrier, inc=1, device_id={"shot": partner}, device_id_type=pl.DeviceIdType.MESH)

    @pl.when(has_up)
    def _():
        pl.semaphore_signal(barrier, inc=1, device_id={"shot": s + 2}, device_id_type=pl.DeviceIdType.MESH)

    @pl.when(has_dn)
    def _():
        pl.semaphore_signal(barrier, inc=1, device_id={"shot": s - 2}, device_id_type=pl.DeviceIdType.MESH)

    pl.semaphore_wait(barrier, subs + has_up.astype(jnp.int32) + has_dn.astype(jnp.int32))

    def tile(c):
        return back.at[c] if c < 3 else lan.at[c - 3]

    gap_copy = remote(gap, gapp, gap_sem, (), {"shot": partner})
    gap_copy.start()
    up_copy = lambda c: remote(tile(c), ub.at[c], zup_sem, (c,), {"shot": s + 2})
    dn_copy = lambda c: remote(tile(c), db.at[c], zdn_sem, (c,), {"shot": s - 2})
    y_copy = lambda c: remote(sb.at[c], yb.at[c], y_sem, (c,), {"shot": partner})

    @pl.when(has_up)
    def _():
        for c in CHANNELS:
            up_copy(c).start()

    @pl.when(jnp.logical_and(even, has_dn))
    def _():
        for c in CHANNELS:
            dn_copy(c).start()

    def zero_plane(ref):
        count, layers = ref.shape[0], ref.shape[1]

        def one(i, carry):
            ref[i // layers, i % layers] = jnp.zeros(ref.shape[2:], jnp.float32)
            return carry

        lax.fori_loop(0, count * layers, one, 0)

    for ref in (bv, bs, av, st, img):
        zero_plane(ref)

    def zero_rim(ref, layer):
        count, layers = ref.shape[0], ref.shape[1]

        def one(i, carry):
            zeros = jnp.zeros((PAD, ref.shape[3]), jnp.float32)
            ref[i // layers, i % layers, 0:PAD] = zeros
            ref[i // layers, i % layers, PAD + rows_y : 2 * PAD + rows_y] = zeros
            return carry

        lax.fori_loop(0, count * layers, one, 0)

    zero_rim(wv, slab)
    zero_rim(ws, 0)

    @pl.when(jnp.logical_not(has_above))
    def _():
        for f in range(3):
            wv[f, slab] = jnp.zeros(wv.shape[2:], jnp.float32)

    @pl.when(jnp.logical_not(has_below))
    def _():
        for f in range(3):
            ws[f, 0] = jnp.zeros(ws.shape[2:], jnp.float32)

    depth = cnt.shape[2]
    receivers = rec_row.shape[1]
    lanes = (rec_col[...] % depth == lax.broadcasted_iota(jnp.int32, (receivers, depth), 1))
    lanes = lanes.astype(jnp.float32).astype(jnp.bfloat16)
    row_of = rec_row[...] // depth

    def count_rows(x, carry):
        rows = lax.broadcasted_iota(jnp.int32, (rows_y, receivers), 0) + x * rows_y
        hot = (rows == row_of).astype(jnp.float32).astype(jnp.bfloat16)
        cnt[x] = jnp.dot(hot, lanes, preferred_element_type=jnp.float32)
        return carry

    lax.fori_loop(0, slab, count_rows, 0)

    for load in loads:
        load.wait()

    ws_rim = lambda: remote(ws.at[pl.ds(0, 3), slab, body], ws.at[pl.ds(0, 3), 0, body], rim_sem, (0,), {"sub": me + 1})
    bs_rim = lambda: remote(bs.at[pl.ds(0, 3), slab, body], bs.at[pl.ds(0, 3), 0, body], rim_sem, (1,), {"sub": me + 1})
    wv_rim = lambda: remote(wv.at[:, 0, body], wv.at[:, slab, body], rim_sem, (2,), {"sub": me - 1})
    bv_rim = lambda: remote(bv.at[:, 0, body], bv.at[:, slab, body], rim_sem, (3,), {"sub": me - 1})
    av_rim = lambda: remote(av.at[:, 0, body], av.at[:, slab, body], rim_sem, (4,), {"sub": me - 1})
    st_rim = lambda: remote(st.at[pl.ds(0, 3), slab, body], st.at[pl.ds(0, 3), 0, body], rim_sem, (5,), {"sub": me + 1})

    def when(*conditions):
        return pl.when(functools.reduce(jnp.logical_and, conditions))

    @pl.when(has_above)
    def _():
        ws_rim().start()

    gap_copy.wait()

    def each_plane(fn):
        def one(i, carry):
            fn(i // slab, i % slab)
            return carry

        lax.fori_loop(0, 2 * slab, one, 0)

    for c in CHANNELS:
        own = tile(c)

        @pl.when(has_dn)
        def _():
            up_copy(c).wait_recv()

        @when(even, has_up)
        def _():
            dn_copy(c).wait_recv()

        @pl.when(even)
        def _():
            each_plane(lambda h, x: sb.__setitem__((c, h, x), jnp.where(gapp[...] == 0.0, db[c, h, x], own[h, x])))

        @pl.when(odd)
        def _():
            each_plane(lambda h, x: sb.__setitem__((c, h, x), jnp.where(gapp[...] == 0.0, own[h, x], ub[c, h, x])))

        y_copy(c).start()

    def q_copy(c, k):
        to = lax.rem(me + k, subs)
        return remote(pp.at[c, to], prm.at[c, :, pl.ds(pl.multiple_of(me * share, 8), share)], q_sem, (c, k), {"sub": to})

    def q_own(c):
        return pltpu.make_async_copy(pp.at[c, me], prm.at[c, :, pl.ds(pl.multiple_of(me * share, 8), share)], loc_sem.at[c])

    for c in CHANNELS:
        own = tile(c)
        y_copy(c).wait_recv()

        def pick(h, x):
            g = gap[...]
            t, y, u = own[h, x], yb[c, h, x], ub[c, h, x]
            pp[c, h, x] = time_step * jnp.where(g == -2.0, u, jnp.where(g == -1.0, y, t))
            pp[c, 2 + h, x] = time_step * jnp.where(g == -1.0, t, y)

        each_plane(pick)
        for k in range(1, subs):
            q_copy(c, k).start()
        q_own(c).start()

    for c in CHANNELS:
        for k in range(1, subs):
            q_copy(c, k).wait()
        q_own(c).wait()
        y_copy(c).wait_send()

        @pl.when(has_up)
        def _():
            up_copy(c).wait_send()

        @when(even, has_dn)
        def _():
            dn_copy(c).wait_send()

    blocks = rows_y // BLOCK
    lane = lax.broadcasted_iota(jnp.int32, (BLOCK, depth), 1)

    def z_lower(v):
        return v - jnp.where(lane == 0, 0.0, pltpu.roll(v, 1, 1))

    def z_upper(v):
        return jnp.where(lane == depth - 1, 0.0, pltpu.roll(v, depth - 1, 1)) - v

    def rows(first, last, fn):
        def one(i, carry):
            x = i // blocks
            fn(x, pl.multiple_of((i % blocks) * BLOCK, BLOCK))
            return carry

        lax.fori_loop(first * blocks, last * blocks, one, 0)

    def accelerate(ref, x, y0):
        at = lambda f, dx, dy: ref[f, x + dx, pl.ds(y0 + PAD + dy, BLOCK), :]
        xx, xy, xz, yy, yz, zz = [at(f, 1, 0) for f in range(6)]
        ax = (xx - at(0, 0, 0)) + (xy - at(1, 1, -1)) + z_lower(xz)
        ay = (xy - at(1, 0, 0)) + (yy - at(3, 1, -1)) + z_lower(yz)
        az = (xz - at(2, 0, 0)) + (yz - at(4, 1, -1)) + z_lower(zz)
        return ax, ay, az

    def strain(ref, x, y0):
        at = lambda f, dx, dy: ref[f, x + dx, pl.ds(y0 + PAD + dy, BLOCK), :]
        vx, vy, vz = [at(f, 0, 0) for f in range(3)]
        normal = (at(0, 1, 0) - vx, at(1, 0, 1) - vy, z_upper(vz))
        shear = (
            (at(0, 0, 1) - vx) + (at(1, 1, 0) - vy),
            z_upper(vx) + (at(2, 1, 0) - vz),
            z_upper(vy) + (at(2, 0, 1) - vz),
        )
        return normal, shear

    def rate(lame, mu, normal, shear):
        first = lame * (normal[0] + normal[1] + normal[2])
        twice = 2.0 * mu
        return (
            first + twice * normal[0], mu * shear[0], mu * shear[1],
            first + twice * normal[1], mu * shear[2], first + twice * normal[2],
        )

    def param(c, x, y0):
        return prm[c, x, pl.ds(y0, BLOCK), :]

    def wave_velocity(t):
        def fn(x, y0):
            accel = accelerate(ws, x, y0)
            buoy = param(2, x, y0)
            for f in range(3):
                hist[t, f, x, pl.ds(y0, BLOCK), :] = accel[f]
                wv[f, x, pl.ds(y0 + PAD, BLOCK), :] += buoy * accel[f]

        return fn

    def born_velocity(t):
        def fn(x, y0):
            accel = accelerate(bs, x, y0)
            buoy, delta = param(2, x, y0), param(5, x, y0)
            for f in range(3):
                new = bv[f, x, pl.ds(y0 + PAD, BLOCK), :] + (
                    buoy * accel[f] + delta * hist[t, f, x, pl.ds(y0, BLOCK), :]
                )
                bv[f, x, pl.ds(y0 + PAD, BLOCK), :] = new
            rec[t, x, pl.ds(y0, BLOCK), :] = cnt[x, pl.ds(y0, BLOCK), :] * new

        return fn

    def wave_stress(t):
        def fn(x, y0):
            normal, shear = strain(wv, x, y0)
            for f in range(3):
                hist[t, 3 + f, x, pl.ds(y0, BLOCK), :] = normal[f]
                hist[t, 6 + f, x, pl.ds(y0, BLOCK), :] = shear[f]
            change = rate(param(0, x, y0), param(1, x, y0), normal, shear)
            for f in range(6):
                ws[f, x + 1, pl.ds(y0 + PAD, BLOCK), :] += change[f]

        return fn

    def born_stress(t):
        def fn(x, y0):
            normal, shear = strain(bv, x, y0)
            change = rate(param(0, x, y0), param(1, x, y0), normal, shear)
            wave_normal = [hist[t, 3 + f, x, pl.ds(y0, BLOCK), :] for f in range(3)]
            wave_shear = [hist[t, 6 + f, x, pl.ds(y0, BLOCK), :] for f in range(3)]
            scatter = rate(param(3, x, y0), param(4, x, y0), wave_normal, wave_shear)
            for f in range(6):
                bs[f, x + 1, pl.ds(y0 + PAD, BLOCK), :] += change[f] + scatter[f]

        return fn

    def forward(t, carry):
        later, more = t > 0, t < STEPS - 1
        rows(1, slab, wave_velocity(t))

        @pl.when(has_below)
        def _():
            ws_rim().wait_recv()

        @when(has_below, later)
        def _():
            wv_rim().wait_send()

        rows(0, 1, wave_velocity(t))

        @pl.when(has_below)
        def _():
            wv_rim().start()

        rows(1, slab, born_velocity(t))

        @when(has_below, later)
        def _():
            bs_rim().wait_recv()
            bv_rim().wait_send()

        rows(0, 1, born_velocity(t))

        @when(has_below, more)
        def _():
            bv_rim().start()

        rows(0, slab - 1, wave_stress(t))

        @pl.when(has_above)
        def _():
            wv_rim().wait_recv()
            ws_rim().wait_send()

        rows(slab - 1, slab, wave_stress(t))

        @when(has_above, more)
        def _():
            ws_rim().start()

        @pl.when(more)
        def _():
            rows(0, slab - 1, born_stress(t))

            @pl.when(has_above)
            def _():
                bv_rim().wait_recv()

            @when(has_above, later)
            def _():
                bs_rim().wait_send()

            rows(slab - 1, slab, born_stress(t))

            @pl.when(has_above)
            def _():
                bs_rim().start()

        return carry

    lax.fori_loop(0, STEPS, forward, 0)

    @pl.when(has_below)
    def _():
        wv_rim().wait_send()

    @pl.when(has_above)
    def _():
        bs_rim().wait_send()

    def adjoint_velocity(t):
        def fn(x, y0):
            accel = accelerate(st, x, y0)
            buoy = param(2, x, y0)
            total = img[2, x, pl.ds(y0, BLOCK), :]
            for f in range(3):
                old = av[f, x, pl.ds(y0 + PAD, BLOCK), :]
                if f == 2:
                    old = old + rec[t, x, pl.ds(y0, BLOCK), :]
                new = old + buoy * accel[f]
                av[f, x, pl.ds(y0 + PAD, BLOCK), :] = new
                total = total + hist[t, f, x, pl.ds(y0, BLOCK), :] * new
            img[2, x, pl.ds(y0, BLOCK), :] = total

        return fn

    def adjoint_stress(t):
        def fn(x, y0):
            normal, shear = strain(av, x, y0)
            change = rate(param(0, x, y0), param(1, x, y0), normal, shear)
            new = []
            for f in range(6):
                new.append(st[f, x + 1, pl.ds(y0 + PAD, BLOCK), :] + change[f])
                st[f, x + 1, pl.ds(y0 + PAD, BLOCK), :] = new[f]
            n0, n1, n2, h0, h1, h2 = [hist[t, 3 + f, x, pl.ds(y0, BLOCK), :] for f in range(6)]
            img[0, x, pl.ds(y0, BLOCK), :] += (n0 + n1 + n2) * (new[0] + new[3] + new[5])
            img[1, x, pl.ds(y0, BLOCK), :] += 2.0 * (n0 * new[0] + n1 * new[3] + n2 * new[5]) + (
                h0 * new[1] + h1 * new[2] + h2 * new[4]
            )

        return fn

    def adjoint(k, carry):
        t = STEPS - 1 - k
        later, more = k > 0, k < STEPS - 1
        rows(1, slab, adjoint_velocity(t))

        @when(has_below, later)
        def _():
            st_rim().wait_recv()
            av_rim().wait_send()

        rows(0, 1, adjoint_velocity(t))

        @pl.when(has_below)
        def _():
            av_rim().start()

        rows(0, slab - 1, adjoint_stress(t))

        @pl.when(has_above)
        def _():
            av_rim().wait_recv()

        @when(has_above, later)
        def _():
            st_rim().wait_send()

        rows(slab - 1, slab, adjoint_stress(t))

        @when(has_above, more)
        def _():
            st_rim().start()

        return carry

    lax.fori_loop(0, STEPS, adjoint, 0)

    @pl.when(has_below)
    def _():
        av_rim().wait_send()

    def g_copy(c, k):
        to = lax.rem(me + k, subs)
        return remote(img.at[c, :, pl.ds(pl.multiple_of(to * share, 8), share)], gb.at[c, me], gq_sem, (c, k), {"sub": to})

    def g_own(c):
        return pltpu.make_async_copy(img.at[c, :, pl.ds(pl.multiple_of(me * share, 8), share)], gb.at[c, me], gloc_sem.at[c])

    gy_copy = lambda c: remote(yout.at[c], yin.at[c], gy_sem, (c,), {"shot": partner})
    gd_copy = lambda c: remote(dout.at[c], din.at[c], gd_sem, (c,), {"shot": s - 2})
    gu_copy = lambda c: remote(uout.at[c], uin.at[c], gu_sem, (c,), {"shot": s + 2})

    for c in (2, 0, 1):
        for k in range(1, subs):
            g_copy(c, k).start()
        g_own(c).start()

    for c in (2, 0, 1):
        for k in range(1, subs):
            g_copy(c, k).wait_recv()
        g_own(c).wait()

        def split(h, x):
            g = gap[...]
            near, far = gb[c, h, x] * time_step, gb[c, 2 + h, x] * time_step
            yout[c, h, x] = jnp.where(g == -1.0, near, far)
            out[c, h, x] = jnp.where(g == -1.0, far, jnp.where(g == 0.0, near, 0.0))
            dout[c, h, x] = jnp.where(g == -2.0, near, 0.0)

        each_plane(split)
        gy_copy(c).start()

    for c in (2, 0, 1):
        gy_copy(c).wait_recv()

        @pl.when(even)
        def _():
            def pass_on(h, x):
                here = gapp[...] <= -1.0
                y = yin[c, h, x]
                out[c, h, x] += jnp.where(here, y, 0.0)
                uout[c, h, x] = jnp.where(here, 0.0, y)

            each_plane(pass_on)

        @pl.when(odd)
        def _():
            def pass_on(h, x):
                here = gapp[...] == 0.0
                y = yin[c, h, x]
                out[c, h, x] += jnp.where(here, y, 0.0)
                dout[c, h, x] += jnp.where(here, 0.0, y)

            each_plane(pass_on)

        @pl.when(has_dn)
        def _():
            gd_copy(c).start()

        @when(even, has_up)
        def _():
            gu_copy(c).start()

    for c in (2, 0, 1):
        @pl.when(has_up)
        def _():
            gd_copy(c).wait_recv()
            each_plane(lambda h, x: out.__setitem__((c, h, x), out[c, h, x] + din[c, h, x]))

        @when(even, has_dn)
        def _():
            gu_copy(c).wait_recv()
            each_plane(lambda h, x: out.__setitem__((c, h, x), out[c, h, x] + uin[c, h, x]))

    for c in (2, 0, 1):
        for k in range(1, subs):
            g_copy(c, k).wait_send()
        gy_copy(c).wait_send()

        @pl.when(has_dn)
        def _():
            gd_copy(c).wait_send()

        @when(even, has_up)
        def _():
            gu_copy(c).wait_send()


def on_device(shots, subs, background, lanczos, incident, receivers, anchors):
    slab, rows_y, depth = incident.shape[2:]
    share = background.shape[2]
    halves = background.shape[1] // slab
    gap = anchors[0] - lax.axis_index("shot")
    gap = jnp.full((share, depth), gap.astype(jnp.float32))
    cut = lambda a: a.reshape(3, halves, slab, share, depth)
    f32 = jnp.float32
    tile = (halves, slab, share, depth)
    plane = (rows_y + 2 * PAD, depth)
    vel, stress = (3, slab + 1) + plane, (6, slab + 1) + plane
    vmem = lambda *shape: pltpu.VMEM(shape, f32)
    dma = lambda *shape: pltpu.SemaphoreType.DMA(shape)
    scratch = [
        vmem(*vel), vmem(*stress), vmem(*vel), vmem(*stress), vmem(*vel), vmem(*stress),
        vmem(STEPS, 9, slab, rows_y, depth), vmem(STEPS, slab, rows_y, depth), vmem(slab, rows_y, depth),
        vmem(6, slab, rows_y, depth), vmem(3, slab, rows_y, depth),
        vmem(share, depth), vmem(6, *tile), vmem(6, *tile), vmem(6, *tile), vmem(6, *tile),
        vmem(6, 2 * halves, slab, share, depth), vmem(3, 2 * halves, slab, share, depth),
        vmem(3, *tile), vmem(3, *tile), vmem(3, *tile), vmem(3, *tile), vmem(3, *tile), vmem(3, *tile),
        dma(9), dma(2), dma(2, 6), dma(2, 6), dma(2, 6), dma(2, 6, subs), dma(6), dma(2, 6),
        dma(2, 3, subs), dma(3), dma(2, 3), dma(2, 3), dma(2, 3),
    ]
    whole = pl.BlockSpec(memory_space=pltpu.VMEM)
    result = pl.pallas_call(
        functools.partial(kernel, shots, subs),
        out_shape=jax.ShapeDtypeStruct((3,) + tile, f32),
        in_specs=[whole, whole, pl.BlockSpec(memory_space=pl.ANY), whole, whole, whole],
        out_specs=whole,
        scratch_shapes=scratch,
        compiler_params=pltpu.CompilerParams(
            collective_id=0, has_side_effects=True, vmem_limit_bytes=60 * 1024 * 1024
        ),
    )(
        cut(background), cut(lanczos), incident[0], gap,
        receivers.reshape(1, -1), receivers.reshape(-1, 1),
    )
    return result.reshape(background.shape)


def solution(mesh):
    placed = (
        P(None, "shot", "sub", None),
        P(None, "shot", "sub", None),
        P("shot", None, "sub", None, None),
        P("shot", "sub", None),
        P("shot"),
    )
    return jax.shard_map(
        functools.partial(on_device, mesh.shape["shot"], mesh.shape["sub"]),
        mesh=mesh,
        in_specs=placed,
        out_specs=P(None, "shot", "sub", None),
        check_vma=False,
    )
```

profile of v0, /device:TPU:0, one launch (start us, length us, event | category | flops | bytes accessed | tf_op | source)
XLA Modules:
  0.0 175.9 jit_solution(6408432738883152413)
XLA Ops:
  0.7 0.6 broadcast_in_dim.3.gap
  1.3 1.5 copy.6.rec_col
  2.7 171.2 %shard_map.55 = f32[3,2,4,48,128]{4,3,2,1,0:T(8,128)} custom-call(f32[3,2,4,48,128]{4,3,2,1,0:T(8,128)} %bitcast.10, f32[3,2,4,48,128]{4,3,2,1,0:T(8,128)} %bitcast.11, f32[9,4,192,128]{3,2,1,0:T(8,128)} %bitcast.8, f32[48,128]{1,0:T(8,128)} %broadcast_in_dim.3.gap, s32[1,256]{1,0:T(1,128)} %bitcast.13, s32[256,1]{1,0:T(8,128)} %copy.6.rec_col), custom_call_target="tpu_custom_call" | custom-call | tf_op jit(solution)/shard_map/pallas_call | solution.py:571
  173.9 1.9 %copy.9 = f32[3,8,48,128]{3,2,1,0:T(8,128)} copy(f32[3,8,48,128]{3,2,1,0:T(8,128)} %bitcast.9) | data formatting | bytes 1179648
where the time goes:
time: 176 us
  Pallas kernels  171 us (97%)
  local copies, waits for them, and re-layouts  3.99 us (2%)
    pallas_call x1, Pallas kernels, on_device(): pl.pallas_call(functools.partial(kernel, shots, subs), out_shape=jax.Shap...  171 us

commit v1 on v0

--- a/solution.py
+++ b/solution.py
@@ -11,6 +11,7 @@
 BLOCK = 32
 PAD = 8
 time_step = 0.25
+WINDOW = 2
 CHANNELS = (2, 5, 0, 1, 3, 4)
 STRESS_FROM = (0, 3, 4, 1, 5, 2)
 
@@ -74,15 +75,17 @@
     dn_copy = lambda c: remote(tile(c), db.at[c], zdn_sem, (c,), {"shot": s - 2})
     y_copy = lambda c: remote(sb.at[c], yb.at[c], y_sem, (c,), {"shot": partner})
 
-    @pl.when(has_up)
-    def _():
-        for c in CHANNELS:
+    def send_tile(c):
+        @pl.when(has_up)
+        def _():
             up_copy(c).start()
 
-    @pl.when(jnp.logical_and(even, has_dn))
-    def _():
-        for c in CHANNELS:
+        @pl.when(jnp.logical_and(even, has_dn))
+        def _():
             dn_copy(c).start()
+
+    for c in CHANNELS[:WINDOW]:
+        send_tile(c)
 
     def zero_plane(ref):
         count, layers = ref.shape[0], ref.shape[1]
@@ -160,7 +163,7 @@
 
         lax.fori_loop(0, 2 * slab, one, 0)
 
-    for c in CHANNELS:
+    def hand_on(c):
         own = tile(c)
 
         @pl.when(has_dn)
@@ -180,6 +183,14 @@
             each_plane(lambda h, x: sb.__setitem__((c, h, x), jnp.where(gapp[...] == 0.0, own[h, x], ub[c, h, x])))
 
         y_copy(c).start()
+
+        @pl.when(has_up)
+        def _():
+            up_copy(c).wait_send()
+
+        @when(even, has_dn)
+        def _():
+            dn_copy(c).wait_send()
 
     def q_copy(c, k):
         to = lax.rem(me + k, subs)
@@ -188,7 +199,7 @@
     def q_own(c):
         return pltpu.make_async_copy(pp.at[c, me], prm.at[c, :, pl.ds(pl.multiple_of(me * share, 8), share)], loc_sem.at[c])
 
-    for c in CHANNELS:
+    def share_out(c):
         own = tile(c)
         y_copy(c).wait_recv()
 
@@ -203,19 +214,10 @@
             q_copy(c, k).start()
         q_own(c).start()
 
-    for c in CHANNELS:
+    def shared(c):
         for k in range(1, subs):
-            q_copy(c, k).wait()
+            q_copy(c, k).wait_recv()
         q_own(c).wait()
-        y_copy(c).wait_send()
-
-        @pl.when(has_up)
-        def _():
-            up_copy(c).wait_send()
-
-        @when(even, has_dn)
-        def _():
-            dn_copy(c).wait_send()
 
     blocks = rows_y // BLOCK
     lane = lax.broadcasted_iota(jnp.int32, (BLOCK, depth), 1)
@@ -287,12 +289,29 @@
 
         return fn
 
+    def born_first(x, y0):
+        delta = param(5, x, y0)
+        for f in range(3):
+            new = delta * hist[0, f, x, pl.ds(y0, BLOCK), :]
+            bv[f, x, pl.ds(y0 + PAD, BLOCK), :] = new
+        rec[0, x, pl.ds(y0, BLOCK), :] = cnt[x, pl.ds(y0, BLOCK), :] * new
+
+    def born_last(x, y0):
+        t = STEPS - 1
+        accel = accelerate(bs, x, y0)[2]
+        new = bv[2, x, pl.ds(y0 + PAD, BLOCK), :] + (
+            param(2, x, y0) * accel + param(5, x, y0) * hist[t, 2, x, pl.ds(y0, BLOCK), :]
+        )
+        rec[t, x, pl.ds(y0, BLOCK), :] = cnt[x, pl.ds(y0, BLOCK), :] * new
+
     def wave_stress(t):
         def fn(x, y0):
             normal, shear = strain(wv, x, y0)
             for f in range(3):
                 hist[t, 3 + f, x, pl.ds(y0, BLOCK), :] = normal[f]
                 hist[t, 6 + f, x, pl.ds(y0, BLOCK), :] = shear[f]
+            if t == STEPS - 1:
+                return
             change = rate(param(0, x, y0), param(1, x, y0), normal, shear)
             for f in range(6):
                 ws[f, x + 1, pl.ds(y0 + PAD, BLOCK), :] += change[f]
@@ -311,79 +330,81 @@
 
         return fn
 
-    def forward(t, carry):
-        later, more = t > 0, t < STEPS - 1
+    def below(*copies):
+        @pl.when(has_below)
+        def _():
+            for act in copies:
+                act()
+
+    def above(*copies):
+        @pl.when(has_above)
+        def _():
+            for act in copies:
+                act()
+
+    def stresses(t):
+        if t == 0:
+            shared(0)
+            shared(1)
+        rows(0, slab - 1, wave_stress(t))
+        above(lambda: wv_rim().wait_recv(), lambda: ws_rim().wait_send())
+        rows(slab - 1, slab, wave_stress(t))
+        if t == STEPS - 1:
+            return
+        above(lambda: ws_rim().start())
+        if t == 0:
+            shared(3)
+            shared(4)
+        rows(0, slab - 1, born_stress(t))
+        above(lambda: bv_rim().wait_recv())
+        if t > 0:
+            above(lambda: bs_rim().wait_send())
+        rows(slab - 1, slab, born_stress(t))
+        above(lambda: bs_rim().start())
+
+    count = len(CHANNELS)
+    for i in range(count + 1):
+        if i < count:
+            hand_on(CHANNELS[i])
+            if i + WINDOW < count:
+                send_tile(CHANNELS[i + WINDOW])
+        if i >= 1:
+            share_out(CHANNELS[i - 1])
+        if i == 3:
+            shared(2)
+            rows(1, slab, wave_velocity(0))
+        if i == 4:
+            below(lambda: ws_rim().wait_recv())
+            rows(0, 1, wave_velocity(0))
+            below(lambda: wv_rim().start())
+        if i == 5:
+            shared(5)
+            rows(0, 1, born_first)
+            below(lambda: bv_rim().start())
+            rows(1, slab, born_first)
+    stresses(0)
+
+    for t in range(1, STEPS):
+        last = t == STEPS - 1
         rows(1, slab, wave_velocity(t))
-
-        @pl.when(has_below)
-        def _():
-            ws_rim().wait_recv()
-
-        @when(has_below, later)
-        def _():
-            wv_rim().wait_send()
-
+        below(lambda: ws_rim().wait_recv(), lambda: wv_rim().wait_send())
         rows(0, 1, wave_velocity(t))
-
-        @pl.when(has_below)
-        def _():
-            wv_rim().start()
-
-        rows(1, slab, born_velocity(t))
-
-        @when(has_below, later)
-        def _():
-            bs_rim().wait_recv()
-            bv_rim().wait_send()
-
-        rows(0, 1, born_velocity(t))
-
-        @when(has_below, more)
-        def _():
-            bv_rim().start()
-
-        rows(0, slab - 1, wave_stress(t))
-
-        @pl.when(has_above)
-        def _():
-            wv_rim().wait_recv()
-            ws_rim().wait_send()
-
-        rows(slab - 1, slab, wave_stress(t))
-
-        @when(has_above, more)
-        def _():
-            ws_rim().start()
-
-        @pl.when(more)
-        def _():
-            rows(0, slab - 1, born_stress(t))
-
-            @pl.when(has_above)
-            def _():
-                bv_rim().wait_recv()
-
-            @when(has_above, later)
-            def _():
-                bs_rim().wait_send()
-
-            rows(slab - 1, slab, born_stress(t))
-
-            @pl.when(has_above)
-            def _():
-                bs_rim().start()
-
-        return carry
-
-    lax.fori_loop(0, STEPS, forward, 0)
-
-    @pl.when(has_below)
-    def _():
-        wv_rim().wait_send()
-
-    @pl.when(has_above)
-    def _():
-        bs_rim().wait_send()
+        below(lambda: wv_rim().start())
+        born = born_last if last else born_velocity(t)
+        rows(1, slab, born)
+        below(lambda: bs_rim().wait_recv(), lambda: bv_rim().wait_send())
+        rows(0, 1, born)
+        if not last:
+            below(lambda: bv_rim().start())
+        stresses(t)
+
+    below(lambda: wv_rim().wait_send())
+    above(lambda: bs_rim().wait_send())
+
+    def adjoint_first(x, y0):
+        new = rec[STEPS - 1, x, pl.ds(y0, BLOCK), :]
+        av[2, x, pl.ds(y0 + PAD, BLOCK), :] = new
+        img[2, x, pl.ds(y0, BLOCK), :] = hist[STEPS - 1, 2, x, pl.ds(y0, BLOCK), :] * new
 
     def adjoint_velocity(t):
         def fn(x, y0):
@@ -417,46 +438,6 @@
 
         return fn
 
-    def adjoint(k, carry):
-        t = STEPS - 1 - k
-        later, more = k > 0, k < STEPS - 1
-        rows(1, slab, adjoint_velocity(t))
-
-        @when(has_below, later)
-        def _():
-            st_rim().wait_recv()
-            av_rim().wait_send()
-
-        rows(0, 1, adjoint_velocity(t))
-
-        @pl.when(has_below)
-        def _():
-            av_rim().start()
-
-        rows(0, slab - 1, adjoint_stress(t))
-
-        @pl.when(has_above)
-        def _():
-            av_rim().wait_recv()
-
-        @when(has_above, later)
-        def _():
-            st_rim().wait_send()
-
-        rows(slab - 1, slab, adjoint_stress(t))
-
-        @when(has_above, more)
-        def _():
-            st_rim().start()
-
-        return carry
-
-    lax.fori_loop(0, STEPS, adjoint, 0)
-
-    @pl.when(has_below)
-    def _():
-        av_rim().wait_send()
-
     def g_copy(c, k):
         to = lax.rem(me + k, subs)
         return remote(img.at[c, :, pl.ds(pl.multiple_of(to * share, 8), share)], gb.at[c, me], gq_sem, (c, k), {"sub": to})
@@ -468,12 +449,39 @@
     gd_copy = lambda c: remote(dout.at[c], din.at[c], gd_sem, (c,), {"shot": s - 2})
     gu_copy = lambda c: remote(uout.at[c], uin.at[c], gu_sem, (c,), {"shot": s + 2})
 
-    for c in (2, 0, 1):
+    def send_image(c):
         for k in range(1, subs):
             g_copy(c, k).start()
         g_own(c).start()
 
-    for c in (2, 0, 1):
+    first_rim = lambda: remote(
+        av.at[pl.ds(2, 1), 0, body], av.at[pl.ds(2, 1), slab, body], rim_sem, (4,), {"sub": me - 1}
+    )
+    for k in range(STEPS):
+        t = STEPS - 1 - k
+        rim = av_rim if k else first_rim
+        if k == 0:
+            rows(0, slab, adjoint_first)
+        else:
+            rows(1, slab, adjoint_velocity(t))
+            below(lambda: st_rim().wait_recv(), lambda: (av_rim if k > 1 else first_rim)().wait_send())
+            rows(0, 1, adjoint_velocity(t))
+        below(lambda: rim().start())
+        rows(0, slab - 1, adjoint_stress(t))
+        if k == STEPS - 1:
+            send_image(2)
+        above(lambda: rim().wait_recv())
+        if k > 0:
+            above(lambda: st_rim().wait_send())
+        rows(slab - 1, slab, adjoint_stress(t))
+        if k < STEPS - 1:
+            above(lambda: st_rim().start())
+
+    below(lambda: av_rim().wait_send())
+    send_image(0)
+    send_image(1)
+
+    def to_partner(c):
         for k in range(1, subs):
             g_copy(c, k).wait_recv()
         g_own(c).wait()
@@ -488,7 +496,7 @@
         each_plane(split)
         gy_copy(c).start()
 
-    for c in (2, 0, 1):
+    def along(c):
         gy_copy(c).wait_recv()
 
         @pl.when(even)
@@ -519,7 +527,7 @@
         def _():
             gu_copy(c).start()
 
-    for c in (2, 0, 1):
+    def collect(c):
         @pl.when(has_up)
         def _():
             gd_copy(c).wait_recv()
@@ -529,6 +537,20 @@
         def _():
             gu_copy(c).wait_recv()
             each_plane(lambda h, x: out.__setitem__((c, h, x), out[c, h, x] + uin[c, h, x]))
+
+    images = (2, 0, 1)
+    for i in range(len(images) + 2):
+        if i < len(images):
+            to_partner(images[i])
+        if 1 <= i <= len(images):
+            along(images[i - 1])
+        if i >= 2:
+            collect(images[i - 2])
+
+    for c in CHANNELS:
+        for k in range(1, subs):
+            q_copy(c, k).wait_send()
+        y_copy(c).wait_send()
 
     for c in (2, 0, 1):
         for k in range(1, subs):

time: 176 us -> 153 us (0.87)
  Pallas kernels: 171 us -> 148 us
    pallas_call x1, Pallas kernels: 171 us -> 148 us  [on_device(): pl.pallas_call(functools.partial(kernel, shots, subs), out_shape=jax.Shap...]
where the time goes in v1:
time: 153 us
  Pallas kernels  148 us (97%)
  local copies, waits for them, and re-layouts  3.99 us (3%)
    pallas_call x1, Pallas kernels, on_device(): pl.pallas_call(functools.partial(kernel, shots, subs), out_shape=jax.Shap...  148 us

profile of v1, /device:TPU:0, one launch (start us, length us, event | category | flops | bytes accessed | tf_op | source)
XLA Modules:
  0.0 153.0 jit_solution(4330796667059620160)
XLA Ops:
  0.7 0.6 broadcast_in_dim.3.gap
  1.3 1.5 copy.6.rec_col
  2.7 148.4 %shard_map.55 = f32[3,2,4,48,128]{4,3,2,1,0:T(8,128)} custom-call(f32[3,2,4,48,128]{4,3,2,1,0:T(8,128)} %bitcast.10, f32[3,2,4,48,128]{4,3,2,1,0:T(8,128)} %bitcast.11, f32[9,4,192,128]{3,2,1,0:T(8,128)} %bitcast.8, f32[48,128]{1,0:T(8,128)} %broadcast_in_dim.3.gap, s32[1,256]{1,0:T(1,128)} %bitcast.13, s32[256,1]{1,0:T(8,128)} %copy.6.rec_col), custom_call_target="tpu_custom_call" | custom-call | tf_op jit(solution)/shard_map/pallas_call | solution.py:593
  151.1 1.9 %copy.9 = f32[3,8,48,128]{3,2,1,0:T(8,128)} copy(f32[3,8,48,128]{3,2,1,0:T(8,128)} %bitcast.9) | data formatting | bytes 1179648
